TPU v7x, 256 devices: a whole 4x4x8 slice. The times are simulated.
256 devices in a mesh: row: 8 (over y, core), col: 32 (over z, x).
Axes of the slice: x: 4, y: 4, z: 8, core: 2. Of those that a mesh axis runs over, the one named last changes fastest.
Arguments:
- probes: bfloat16 [32, 8, 128, 4096], P(None, None, 'row', 'col'), may hold values from -8 to 8
- spread: float32 [8, 128, 4096], P(None, 'row', 'col'), may hold values from 0.05 to 6.5, as said below
- adv_x: float32 [8, 128, 4096], P(None, 'row', 'col'), may hold values from -0.6 to 0.6
- adv_y: float32 [8, 128, 4096], P(None, 'row', 'col'), may hold values from -0.6 to 0.6
- diffusivity: float32 [8, 128, 4096], P(None, 'row', 'col'), may hold values from 0.02 to 0.2
Outputs:
- basis: float32 [32, 8, 128, 4096], P(None, None, 'row', 'col')
- core_factor: float32 [32, 32], replicated
Inputs may be any that keep to these rules, and one draw needn't show every extreme that they name: `spread`: positive everywhere; a rough factor times a scale that varies over the grid.
All inputs are finite; a program needn't handle non-finite values.
Results may differ from a plain program's by a relative error of at most 0.0003.
Values sent between devices are 32-bit elements; how exact they have to be, the bound alone decides.
A program may use at most 128 MiB of HBM per device.

v0:
```python
import functools

import jax
import jax.numpy as jnp
from jax import lax
from jax.experimental import pallas as pl
from jax.experimental.pallas import tpu as pltpu
from jax.sharding import PartitionSpec as P

MESH = pl.DeviceIdType.MESH
F32 = jnp.float32
BF16 = jnp.bfloat16
INNER = 4
WIDTH = 8
GROUP = 2
NF = 8
SPR, CEN, XP, XM, XA, YP, YM, YA = range(NF)
LOW, HIGH, LEFT, RIGHT = range(4)


def lanes(shape):
    return lax.broadcasted_iota(jnp.int32, shape, 1)


def roll(x, shift):
    return pltpu.roll(x, shift % 128, 1)


def put_row(ref, r, value):
    n, rows, width = ref.shape
    ref.reshape(n * rows, width)[pl.ds(r, n, stride=rows), :] = value


def wide(coef, nprobe):
    return jnp.broadcast_to(coef[None], (nprobe // 8, 8, 128)).reshape(nprobe, 128)


def halo_kernel(
    dims,
    probes_hbm, spread_hbm, advx_hbm, advy_hbm, diff_hbm,
    z_hbm, g_ref,
    probes, coefs, turn, omega, scaled, tang, co, edge,
    pack, pack_l, pack_r, wrap, wrap_l, wrap_r,
    to_low, to_high, from_low, from_high,
    back, strip, zbuf, gbuf, red_a, red_b, red_c, total,
    in_sem, out_sem, send_sem, recv_sem, red_send, red_recv,
):
    nprobe, nlev, nrow, nrd, ncd = dims
    outer = ncd // INNER
    row = lax.axis_index("row")
    col = lax.axis_index("col")
    zi = col // INNER
    xi = lax.rem(col, INNER)
    half = nprobe // 2

    loads = []
    for i, src in enumerate((spread_hbm, advx_hbm, advy_hbm, diff_hbm)):
        loads.append(pltpu.make_async_copy(src, coefs.at[i], in_sem.at[i]))
    loads.append(pltpu.make_async_copy(probes_hbm, probes, in_sem.at[4]))
    for load in loads:
        load.start()

    core = lax.rem(row, 2)
    chip = (row // 2) * INNER + xi
    plane = (nrd // 2) * INNER

    def in_plane(t):
        return ((t // INNER) * 2 + core, zi * INNER + lax.rem(t, INNER))

    def in_line(t):
        return (row, t * INNER + xi)

    other = (row + 1 - 2 * core, col)
    barrier = pltpu.get_barrier_semaphore()
    greet = [other]
    greet += [(lax.rem(row + o, nrd), col) for o in (1, nrd - 1)]
    greet += [(row, lax.rem(col + o, ncd)) for o in (1, ncd - 1)]
    greet += [in_plane(lax.rem(chip + o, plane)) for o in range(1, plane)]
    greet += [in_line(lax.rem(zi + o, outer)) for o in range(1, outer)]
    for device in greet:
        pl.semaphore_signal(barrier, inc=1, device_id=device, device_id_type=MESH)
    signals = len(greet)

    for load in loads[:4]:
        load.wait()

    def spread_coefs(l, carry):
        ax = coefs[1, l] * (1.0 / 12.0)
        ay = coefs[2, l] * (1.0 / 12.0)
        d = coefs[3, l]
        fields = (coefs[0, l], 0.6 - 4.0 * d, d + 8.0 * ax, d - 8.0 * ax, ax, d + 8.0 * ay, d - 8.0 * ay, ay)
        for f in range(NF):
            for r in range(nrow):
                co[f, l, r] = jnp.broadcast_to(fields[f][r : r + 1], (8, 128))
        return carry

    lax.fori_loop(0, nlev, spread_coefs, 0)

    lane16 = lanes((half, 128))
    quad = lax.rem(lane16, 4)
    lane_l = lanes((nlev, 128))
    quad_l = lax.rem(lane_l, 4)

    def packed(field):
        acc = jnp.zeros((nlev, 128), F32)
        for r in range(nrow):
            acc = jnp.where(lax.div(lane_l, 4) == r, roll(coefs[field, :, r, :], 4 * r + 2), acc)
        return jnp.where(lane_l < 64, acc, roll(acc, 64))

    pa = packed(2) * (1.0 / 12.0)
    pd = packed(3)
    edge[0] = jnp.where(quad_l == 1, pd + 8.0 * pa, jnp.where(quad_l == 2, pd - 8.0 * pa, 0.0))
    edge[1] = pa

    has = {LOW: row > 0, HIGH: row < nrd - 1, LEFT: col > 0, RIGHT: col < ncd - 1}
    target = {LOW: (row - 1, col), HIGH: (row + 1, col), LEFT: (row, col - 1), RIGHT: (row, col + 1)}
    rims = (
        {
            LOW: (lambda l: scaled.at[l, 2:4], lambda l: scaled.at[l, nrow + 2 : nrow + 4]),
            HIGH: (lambda l: scaled.at[l, nrow : nrow + 2], lambda l: scaled.at[l, 0:2]),
            LEFT: (lambda l: pack.at[l], lambda l: pack_r.at[l]),
            RIGHT: (lambda l: pack.at[l], lambda l: pack_l.at[l]),
        },
        {
            LOW: (lambda l: to_low.at[l], lambda l: from_high.at[l]),
            HIGH: (lambda l: to_high.at[l], lambda l: from_low.at[l]),
            LEFT: (lambda l: wrap.at[l], lambda l: wrap_r.at[l]),
            RIGHT: (lambda l: wrap.at[l], lambda l: wrap_l.at[l]),
        },
    )
    opposite = {LOW: HIGH, HIGH: LOW, LEFT: RIGHT, RIGHT: LEFT}

    def rim(phase, side, l):
        src, dst = rims[phase][side]
        return pltpu.make_async_remote_copy(
            src_ref=src(l),
            dst_ref=dst(l),
            send_sem=send_sem.at[phase, side, l],
            recv_sem=recv_sem.at[phase, side, l],
            device_id=target[side],
            device_id_type=MESH,
        )

    def send(phase, l):
        for side in (LOW, HIGH, LEFT, RIGHT):
            @pl.when(has[side])
            def _():
                rim(phase, side, l).start()

    def receive(phase, l):
        for side in (LEFT, RIGHT, LOW, HIGH):
            @pl.when(has[side])
            def _():
                rim(phase, opposite[side], l).wait_recv()

    def sent(phase, l):
        for side in (LOW, HIGH, LEFT, RIGHT):
            @pl.when(has[side])
            def _():
                rim(phase, side, l).wait_send()

    zero_rows = jnp.zeros((nlev, 2, nprobe, 128), F32)
    zero_pack = jnp.zeros((nlev, half, 128), F32)

    @pl.when(row == 0)
    def _():
        scaled[:, 0:2] = zero_rows
        from_low[...] = zero_rows

    @pl.when(row == nrd - 1)
    def _():
        scaled[:, nrow + 2 : nrow + 4] = zero_rows
        from_high[...] = zero_rows

    @pl.when(col == 0)
    def _():
        pack_l[...] = zero_pack
        wrap_l[...] = zero_pack

    @pl.when(col == ncd - 1)
    def _():
        pack_r[...] = zero_pack
        wrap_r[...] = zero_pack

    loads[4].wait()

    def put(acc, r, value):
        slot = lax.div(lane16, 4)
        acc = jnp.where(slot == r, roll(value[:half], 4 * r + 2), acc)
        return jnp.where(slot == r + 16, roll(value[half:], 4 * r + 66), acc)

    wide_lane = lanes((nprobe, 128))
    at_edge = jnp.logical_or(wide_lane < 2, wide_lane >= 126)

    def take(corr, r):
        both = jnp.concatenate([roll(corr, -(4 * r + 2)), roll(corr, -(4 * r + 66))], axis=0)
        return jnp.where(at_edge, both, 0.0)

    def scale_level(l, carry):
        for p in range(nprobe):
            turn[p * nrow : (p + 1) * nrow, :] = probes[p, l].astype(F32)
        acc = jnp.zeros((half, 128), F32)
        for r in range(nrow):
            om = turn[pl.ds(r, nprobe, stride=nrow), :]
            omega[l, r] = om.astype(BF16)
            v = om * wide(co[SPR, l, r], nprobe)
            scaled[l, r + 2] = v
            acc = put(acc, r, v)
        pack[l] = acc
        return carry

    lax.fori_loop(0, nlev, scale_level, 0)

    pl.semaphore_wait(barrier, signals)

    def send_level(l, carry):
        send(0, l)
        return carry

    lax.fori_loop(0, nlev, send_level, 0)

    def tangent_row(l, r):
        above = jnp.minimum(l + 1, nlev - 1)
        below = jnp.maximum(l - 1, 0)
        c = [wide(co[f, l, r], nprobe) for f in range(NF)]
        v = scaled[l, r + 2]
        t = c[CEN] * v + 0.2 * (scaled[above, r + 2] + scaled[below, r + 2])
        t = t + c[XP] * scaled[l, r + 3] + c[XM] * scaled[l, r + 1]
        t = t + c[XA] * (scaled[l, r] - scaled[l, r + 4])
        return t + c[YP] * roll(v, -1) + c[YM] * roll(v, 1) + c[YA] * (roll(v, 2) - roll(v, -2))

    def tangent_inner(l, carry):
        for r in range(2, nrow - 2):
            tang[l, r] = tangent_row(l, r)
        return carry

    def gather(l, carry):
        acc = jnp.zeros((half, 128), F32)
        for r in range(2, nrow - 2):
            acc = put(acc, r, tang[l, r])
        strip[l] = acc
        return carry

    lax.fori_loop(0, nlev, tangent_inner, 0)
    lax.fori_loop(0, nlev, gather, 0)

    def tangent_outer(l):
        e1 = edge[0, pl.ds(l, 1), :]
        ea = edge[1, pl.ds(l, 1), :]
        diff = jnp.where(quad < 2, pack_l[l], pack_r[l]) - pack[l]
        near = jnp.where(quad == 1, roll(diff, -1), roll(diff, 1))
        far = jnp.where(quad < 2, -roll(diff, -2), roll(diff, 2))
        corr = e1 * near + ea * far
        acc = strip[l] + corr
        ends = {}
        for r in (0, 1, nrow - 2, nrow - 1):
            t = tangent_row(l, r) + take(corr, r)
            tang[l, r] = t
            ends[r] = t
            acc = put(acc, r, t)
        last = nrow - 1

        def coef(f, r):
            return wide(co[f, l, r], nprobe)

        to_low[l, 0] = coef(XA, 0) * ends[0]
        to_low[l, 1] = coef(XM, 0) * ends[0] + coef(XA, 1) * ends[1]
        to_high[l, 0] = coef(XP, last) * ends[last] - coef(XA, last - 1) * ends[last - 1]
        to_high[l, 1] = -(coef(XA, last) * ends[last])
        u = ea * acc
        w = e1 * acc
        wrap[l] = jnp.where(quad < 2, roll(u, -2), -roll(u, 2)) + jnp.where(
            quad == 1, roll(w, -1), jnp.where(quad == 2, roll(w, 1), 0.0)
        )
        for r in range(2, nrow - 2):
            tang[l, r] = tang[l, r] + take(corr, r)

    def tangent_rims(g, carry):
        group = [g * GROUP + i for i in range(GROUP)]
        for l in group:
            receive(0, l)
        for l in group:
            tangent_outer(l)
        for l in group:
            send(1, l)
        return carry

    lax.fori_loop(0, nlev // GROUP, tangent_rims, 0)

    def adjoint_own(l, carry):
        above = jnp.minimum(l + 1, nlev - 1)
        below = jnp.maximum(l - 1, 0)
        for r in range(nrow):
            c = [wide(co[f, l, r], nprobe) for f in (CEN, YP, YM, YA)]
            w = tang[l, r]
            b = c[0] * w + 0.2 * (tang[above, r] + tang[below, r])
            if r + 1 < nrow:
                b = b + wide(co[XM, l, r + 1], nprobe) * tang[l, r + 1]
            if r >= 1:
                b = b + wide(co[XP, l, r - 1], nprobe) * tang[l, r - 1]
            if r + 2 < nrow:
                b = b + wide(co[XA, l, r + 2], nprobe) * tang[l, r + 2]
            if r >= 2:
                b = b - wide(co[XA, l, r - 2], nprobe) * tang[l, r - 2]
            ya = c[3] * w
            back[l, r] = b + roll(c[2] * w, -1) + roll(c[1] * w, 1) + (roll(ya, -2) - roll(ya, 2))
        return carry

    lax.fori_loop(0, nlev, adjoint_own, 0)

    def sketch_level(l):
        corr = jnp.where(quad < 2, wrap_r[l], wrap_l[l]) - wrap[l]
        left, right = [], []
        for r in range(nrow):
            b = back[l, r] + take(corr, r)
            if r < 2:
                b = b + from_low[l, r]
            if r >= nrow - 2:
                b = b + from_high[l, r - (nrow - 2)]
            om = omega[l, r]
            sk = om.astype(F32) + wide(co[SPR, l, r], nprobe) * b
            hi = sk.astype(BF16)
            lo = (sk - hi.astype(F32)).astype(BF16)
            z = jnp.concatenate([hi, lo], axis=0)
            zbuf[l, r] = z
            right.append(z)
            left.append(jnp.concatenate([hi, om], axis=0))
        return lax.dot_general(
            jnp.concatenate(left, axis=1),
            jnp.concatenate(right, axis=1),
            (((1,), (1,)), ((), ())),
            preferred_element_type=F32,
        )

    def sketch_rims(g, gram):
        group = [g * GROUP + i for i in range(GROUP)]
        for l in group:
            receive(1, l)
        for l in group:
            gram = gram + sketch_level(l)
        for l in group:
            pltpu.make_async_copy(zbuf.at[l], z_hbm.at[l], out_sem.at[l]).start()
        return gram

    gram = lax.fori_loop(0, nlev // GROUP, sketch_rims, jnp.zeros((2 * nprobe, 2 * nprobe), F32))

    gbuf[...] = jnp.zeros(gbuf.shape, F32)
    gbuf[:, 0 : 2 * nprobe] = gram
    full = gbuf[...]
    high, probe = full[:nprobe], full[nprobe:]
    own = high + 2.0 * roll(high, -nprobe)
    both = jnp.where(wide_lane < nprobe, own, roll(probe, nprobe) + probe)
    part = jnp.where(lane16 < 64, both[:half], roll(both[half:], 64))

    pair_part = red_a
    pair_part[0] = part
    swap = pltpu.make_async_remote_copy(
        src_ref=pair_part.at[0], dst_ref=pair_part.at[1], send_sem=red_send.at[0, 0], recv_sem=red_recv.at[0, 0],
        device_id=other, device_id_type=MESH,
    )
    swap.start()
    swap.wait_recv()
    quarter = half // 2
    mine = pl.ds(pl.multiple_of(core * quarter, quarter), quarter)
    part = pair_part[0, mine] + pair_part[1, mine]
    copies = [swap]
    for s, (buf, count, me, at) in enumerate(((red_b, plane, chip, in_plane), (red_c, outer, zi, in_line))):
        buf[me] = part
        stage = []
        for o in range(1, count):
            stage.append(
                pltpu.make_async_remote_copy(
                    src_ref=buf.at[me],
                    dst_ref=buf.at[me],
                    send_sem=red_send.at[s + 1, o],
                    recv_sem=red_recv.at[s + 1, o],
                    device_id=at(lax.rem(me + o, count)),
                    device_id_type=MESH,
                )
            )
            stage[-1].start()
        for copy in stage:
            copy.wait_recv()
        terms = [buf[o] for o in range(count)]
        while len(terms) > 1:
            terms = [sum(terms[i : i + 2][1:], terms[i]) for i in range(0, len(terms), 2)]
        part = terms[0]
        copies += stage
    total[mine] = part
    join = pltpu.make_async_remote_copy(
        src_ref=total.at[mine], dst_ref=total.at[mine], send_sem=red_send.at[0, 1], recv_sem=red_recv.at[0, 1],
        device_id=other, device_id_type=MESH,
    )
    join.start()
    join.wait_recv()
    copies.append(join)
    g_ref[...] = total[...]

    for copy in copies:
        copy.wait_send()

    def finish(l, carry):
        sent(0, l)
        sent(1, l)
        pltpu.make_async_copy(zbuf.at[l], z_hbm.at[l], out_sem.at[l]).wait()
        return carry

    lax.fori_loop(0, nlev, finish, 0)


def basis_kernel(nprobe, nlev, nrow, scale, g_ref, z_hbm, basis_hbm, factor_ref, zbuf, obuf, in_sem, out_sem):
    def load(l):
        return pltpu.make_async_copy(z_hbm.at[l], zbuf.at[l], in_sem.at[l])

    def store(l):
        return pltpu.make_async_copy(obuf.at[l], basis_hbm.at[:, l], out_sem.at[l])

    for l in range(nlev):
        load(l).start()
    half = nprobe // 2
    g = g_ref[...]
    both = jnp.concatenate([g, roll(g, 64)], axis=0)
    flip = both.T
    lane = lanes((nprobe, 128))
    sub = lax.broadcasted_iota(jnp.int32, (nprobe, 128), 0)
    pad = jnp.zeros((nprobe, 128 - nprobe), F32)
    flip_g = jnp.concatenate([flip[:nprobe], pad], axis=1)
    flip_c = jnp.concatenate([flip[nprobe : 2 * nprobe], pad], axis=1)
    sym_g = 0.5 * (both + flip_g)
    sym_c = 0.5 * (roll(both, -nprobe) + flip_c)
    m = jnp.where(lane < nprobe, sym_g, jnp.where(jnp.logical_and(lane >= 64, lane < 64 + nprobe), roll(sym_c, 64), 0.0))
    m = jnp.where(jnp.logical_or(lane == sub + nprobe, lane == sub + 64 + nprobe), 1.0, m)
    first = lane < 64
    piv = jnp.ones((nprobe, 128), F32)
    for k0 in range(0, nprobe, WIDTH):
        cols = [
            jnp.where(
                first,
                jnp.broadcast_to(m[:, k : k + 1], (nprobe, 128)),
                jnp.broadcast_to(m[:, 64 + k : 65 + k], (nprobe, 128)),
            )
            for k in range(k0, k0 + WIDTH)
        ]
        for j in range(WIDTH):
            k = k0 + j
            p = cols[j][k : k + 1]
            inv = 1.0 / p
            piv = jnp.where(sub == k, p, piv)
            below = jnp.where(sub > k, cols[j], 0.0)
            for i in range(j + 1, WIDTH):
                cols[i] = cols[i] - below * (cols[i][k : k + 1] * inv)
            m = m - below * (m[k : k + 1] * inv)
    m = m * (1.0 / jnp.sqrt(piv))
    upper = jnp.where(jnp.logical_and(lane >= sub, lane < nprobe), m, 0.0)
    inv_g = jnp.where(lane <= sub, roll(m, -nprobe), 0.0)
    inv_c = jnp.where(lane <= sub, roll(m, -(64 + nprobe)), 0.0)
    factor = lax.dot_general(
        upper, inv_c, (((1,), (1,)), ((), ())), precision=lax.Precision.HIGHEST, preferred_element_type=F32
    )
    factor_ref[...] = factor
    a = inv_g * scale
    a_hi = a.astype(BF16)
    a_lo = (a - a_hi.astype(F32)).astype(BF16)
    twice = jnp.where(lane < nprobe, a_hi.astype(F32), roll(a_hi.astype(F32), nprobe))
    twice_lo = jnp.where(lane < nprobe, a_lo.astype(F32), roll(a_lo.astype(F32), nprobe))
    lhs = jnp.concatenate([twice, twice_lo], axis=0).astype(BF16)[:, : 2 * nprobe]

    def level(l, carry):
        load(l).wait()
        for r in range(0, nrow, 2):
            out = lax.dot_general(
                lhs,
                jnp.concatenate([zbuf[l, r], zbuf[l, r + 1]], axis=1),
                (((1,), (0,)), ((), ())),
                preferred_element_type=F32,
            )
            out = out[:nprobe] + out[nprobe:]
            put_row(obuf.at[l], r, out[:, :128])
            put_row(obuf.at[l], r + 1, out[:, 128:])
        store(l).start()
        return carry

    lax.fori_loop(0, nlev, level, 0)

    def finish(l, carry):
        store(l).wait()
        return carry

    lax.fori_loop(0, nlev, finish, 0)


def shards(probes, spread, adv_x, adv_y, diffusivity):
    nprobe, nlev, nrow, ncol = probes.shape
    nrd = lax.axis_size("row")
    ncd = lax.axis_size("col")
    half = nprobe // 2
    inputs = [pltpu.with_memory_space_constraint(x, pltpu.HBM) for x in (probes, spread, adv_x, adv_y, diffusivity)]
    any_spec = pl.BlockSpec(memory_space=pltpu.HBM)
    vmem_spec = pl.BlockSpec(memory_space=pltpu.VMEM)
    rows2 = pltpu.VMEM((nlev, 2, nprobe, ncol), F32)
    strip = pltpu.VMEM((nlev, half, ncol), F32)
    plane = (nrd // 2) * INNER
    most = max(2, plane, ncd // INNER)
    z, g = pl.pallas_call(
        functools.partial(halo_kernel, (nprobe, nlev, nrow, nrd, ncd)),
        out_shape=(
            jax.ShapeDtypeStruct((nlev, nrow, 2 * nprobe, ncol), BF16),
            jax.ShapeDtypeStruct((half, ncol), F32),
        ),
        in_specs=[any_spec] * 5,
        out_specs=(any_spec, vmem_spec),
        scratch_shapes=[
            pltpu.VMEM((nprobe, nlev, nrow, ncol), BF16),
            pltpu.VMEM((4, nlev, nrow, ncol), F32),
            pltpu.VMEM((nprobe * nrow, ncol), F32),
            pltpu.VMEM((nlev, nrow, nprobe, ncol), BF16),
            pltpu.VMEM((nlev, nrow + 4, nprobe, ncol), F32),
            pltpu.VMEM((nlev, nrow, nprobe, ncol), F32),
            pltpu.VMEM((NF, nlev, nrow, 8, ncol), F32),
            pltpu.VMEM((2, nlev, ncol), F32),
            strip, strip, strip, strip, strip, strip,
            rows2, rows2, rows2, rows2,
            pltpu.VMEM((nlev, nrow, nprobe, ncol), F32),
            strip,
            pltpu.VMEM((nlev, nrow, 2 * nprobe, ncol), BF16),
            pltpu.VMEM((2 * nprobe, ncol), F32),
            pltpu.VMEM((2, half, ncol), F32),
            pltpu.VMEM((plane, half // 2, ncol), F32),
            pltpu.VMEM((ncd // INNER, half // 2, ncol), F32),
            pltpu.VMEM((half, ncol), F32),
            pltpu.SemaphoreType.DMA((5,)),
            pltpu.SemaphoreType.DMA((nlev,)),
            pltpu.SemaphoreType.DMA((2, 4, nlev)),
            pltpu.SemaphoreType.DMA((2, 4, nlev)),
            pltpu.SemaphoreType.DMA((3, most)),
            pltpu.SemaphoreType.DMA((3, most)),
        ],
        compiler_params=pltpu.CompilerParams(
            collective_id=0, has_side_effects=True, vmem_limit_bytes=40 * 1024 * 1024
        ),
        name="sketch_and_sums",
    )(*inputs)
    scale = float(nlev * nrow * ncol * nrd * ncd) ** 0.5
    basis, factor = pl.pallas_call(
        functools.partial(basis_kernel, nprobe, nlev, nrow, scale),
        out_shape=(
            jax.ShapeDtypeStruct((nprobe, nlev, nrow, ncol), F32),
            jax.ShapeDtypeStruct((nprobe, nprobe), F32),
        ),
        in_specs=[vmem_spec, any_spec],
        out_specs=(any_spec, vmem_spec),
        scratch_shapes=[
            pltpu.VMEM((nlev, nrow, 2 * nprobe, ncol), BF16),
            pltpu.VMEM((nlev, nprobe, nrow, ncol), F32),
            pltpu.SemaphoreType.DMA((nlev,)),
            pltpu.SemaphoreType.DMA((nlev,)),
        ],
        compiler_params=pltpu.CompilerParams(vmem_limit_bytes=24 * 1024 * 1024),
        name="factors_and_basis",
    )(g, z)
    return basis, factor


def solution(mesh):
    return jax.shard_map(
        shards,
        mesh=mesh,
        in_specs=(
            P(None, None, "row", "col"),
            P(None, "row", "col"),
            P(None, "row", "col"),
            P(None, "row", "col"),
            P(None, "row", "col"),
        ),
        out_specs=(P(None, None, "row", "col"), P()),
        check_vma=False,
    )
```

profile of v0, /device:TPU:1, one launch (start us, length us, event | category | flops | bytes accessed | tf_op | source)
XLA Modules:
  0.0 40.5 jit_solution(12988120866788424352)
XLA Ops:
  0.6 35.2 %sketch_and_sums.1 = (bf16[8,16,64,128]{3,2,1,0:T(8,128)(2,1)S(1)}, f32[16,128]{1,0:T(8,128)S(1)}) custom-call(bf16[32,8,16,128]{3,2,1,0:T(8,128)(2,1)} %probes_hbm.1, f32[8,16,128]{2,1,0:T(8,128)} %spread_hbm.1, f32[8,16,128]{2,1,0:T(8,128)} %advx_hbm.1, f32[8,16,128]{2,1,0:T(8,128)} %advy_hbm.1, f32[8,16,128]{2,1,0:T(8,128)} %diff_hbm.1), custom_call_target="tpu_custom_call" | custom-call | tf_op jit(solution)/shard_map/sketch_and_sums/pallas_call | solution.py:504
  35.9 4.6 %factors_and_basis.1 = (f32[32,8,16,128]{3,2,1,0:T(8,128)}, f32[32,32]{1,0:T(8,128)}) custom-call(f32[16,128]{1,0:T(8,128)S(1)} %get-tuple-element.4.g_ref, bf16[8,16,64,128]{3,2,1,0:T(8,128)(2,1)S(1)} %get-tuple-element.5.z_hbm), custom_call_target="tpu_custom_call" | custom-call | tf_op jit(solution)/shard_map/factors_and_basis/pallas_call | solution.py:544
where the time goes:
time: 40.6 us; the launch traced here: 40.5 us
  Pallas kernels  39.8 us (98%)
  between operations  0.64 us (2%)
    pallas_call x1, Pallas kernels, shards(): pl.pallas_call(functools.partial(halo_kernel, (nprobe, nlev, nrow, nrd, n...  35.2 us
    pallas_call x1, Pallas kernels, shards(): pl.pallas_call(functools.partial(basis_kernel, nprobe, nlev, nrow, scale)...  4.62 us

commit v1 on v0

--- a/solution.py
+++ b/solution.py
@@ -12,9 +12,10 @@
 BF16 = jnp.bfloat16
 INNER = 4
 WIDTH = 8
+CHUNK = 8
 GROUP = 2
-NF = 8
-SPR, CEN, XP, XM, XA, YP, YM, YA = range(NF)
+NF = 7
+SPR, CEN, XP, XM, XA, YA, DIF = range(NF)
 LOW, HIGH, LEFT, RIGHT = range(4)
 
 
@@ -39,7 +40,7 @@
     dims,
     probes_hbm, spread_hbm, advx_hbm, advy_hbm, diff_hbm,
     z_hbm, g_ref,
-    probes, coefs, turn, omega, scaled, tang, co, edge,
+    probes, coefs, turn, omega, scaled, tang, co, edge, ring, ring_t,
     pack, pack_l, pack_r, wrap, wrap_l, wrap_r,
     to_low, to_high, from_low, from_high,
     back, strip, zbuf, gbuf, red_a, red_b, red_c, total,
@@ -88,7 +89,7 @@
         ax = coefs[1, l] * (1.0 / 12.0)
         ay = coefs[2, l] * (1.0 / 12.0)
         d = coefs[3, l]
-        fields = (coefs[0, l], 0.6 - 4.0 * d, d + 8.0 * ax, d - 8.0 * ax, ax, d + 8.0 * ay, d - 8.0 * ay, ay)
+        fields = (coefs[0, l], 0.6 - 4.0 * d, d + 8.0 * ax, d - 8.0 * ax, ax, ay, d)
         for f in range(NF):
             for r in range(nrow):
                 co[f, l, r] = jnp.broadcast_to(fields[f][r : r + 1], (8, 128))
@@ -111,6 +112,18 @@
     pd = packed(3)
     edge[0] = jnp.where(quad_l == 1, pd + 8.0 * pa, jnp.where(quad_l == 2, pd - 8.0 * pa, 0.0))
     edge[1] = pa
+
+    for k, shape in enumerate(((256, 256), (512, 128))):
+        src_lane = lax.rem(lax.broadcasted_iota(jnp.int32, shape, 0), 128)
+        src_part = lax.div(lax.broadcasted_iota(jnp.int32, shape, 0), 128)
+        out_col = lax.broadcasted_iota(jnp.int32, shape, 1)
+        step = lax.rem(src_lane - lax.rem(out_col, 128) + 128, 128)
+        first = jnp.where(step == 1, 8.0, jnp.where(step == 127, -8.0, jnp.where(step == 2, -1.0, jnp.where(step == 126, 1.0, 0.0))))
+        both = jnp.where(jnp.logical_or(step == 1, step == 127), 1.0, 0.0)
+        if k == 0:
+            ring[...] = jnp.where(out_col < 128, first, both).astype(BF16)
+        else:
+            ring_t[...] = jnp.where(src_part < 2, both, -first).astype(BF16)
 
     has = {LOW: row > 0, HIGH: row < nrd - 1, LEFT: col > 0, RIGHT: col < ncd - 1}
     target = {LOW: (row - 1, col), HIGH: (row + 1, col), LEFT: (row, col - 1), RIGHT: (row, col + 1)}
@@ -183,6 +196,7 @@
         wrap_r[...] = zero_pack
 
     loads[4].wait()
+    pl.semaphore_wait(barrier, signals)
 
     def put(acc, r, value):
         slot = lax.div(lane16, 4)
@@ -196,7 +210,7 @@
         both = jnp.concatenate([roll(corr, -(4 * r + 2)), roll(corr, -(4 * r + 66))], axis=0)
         return jnp.where(at_edge, both, 0.0)
 
-    def scale_level(l, carry):
+    def scale_level(l, turn):
         for p in range(nprobe):
             turn[p * nrow : (p + 1) * nrow, :] = probes[p, l].astype(F32)
         acc = jnp.zeros((half, 128), F32)
@@ -207,42 +221,52 @@
             scaled[l, r + 2] = v
             acc = put(acc, r, v)
         pack[l] = acc
-        return carry
-
-    lax.fori_loop(0, nlev, scale_level, 0)
-
-    pl.semaphore_wait(barrier, signals)
-
-    def send_level(l, carry):
-        send(0, l)
-        return carry
-
-    lax.fori_loop(0, nlev, send_level, 0)
-
-    def tangent_row(l, r):
+
+    def scale_group(g, carry):
+        group = [g * GROUP + i for i in range(GROUP)]
+        for i, l in enumerate(group):
+            scale_level(l, turn.at[i])
+        for l in group:
+            send(0, l)
+        return carry
+
+    lax.fori_loop(0, nlev // GROUP, scale_group, 0)
+
+    def halves(x):
+        high = x.astype(BF16)
+        return high, (x - high.astype(F32)).astype(BF16)
+
+    def tangent_own(l, carry):
         above = jnp.minimum(l + 1, nlev - 1)
         below = jnp.maximum(l - 1, 0)
-        c = [wide(co[f, l, r], nprobe) for f in range(NF)]
-        v = scaled[l, r + 2]
-        t = c[CEN] * v + 0.2 * (scaled[above, r + 2] + scaled[below, r + 2])
-        t = t + c[XP] * scaled[l, r + 3] + c[XM] * scaled[l, r + 1]
-        t = t + c[XA] * (scaled[l, r] - scaled[l, r + 4])
-        return t + c[YP] * roll(v, -1) + c[YM] * roll(v, 1) + c[YA] * (roll(v, 2) - roll(v, -2))
-
-    def tangent_inner(l, carry):
-        for r in range(2, nrow - 2):
-            tang[l, r] = tangent_row(l, r)
-        return carry
-
-    def gather(l, carry):
         acc = jnp.zeros((half, 128), F32)
-        for r in range(2, nrow - 2):
-            acc = put(acc, r, tang[l, r])
+        for r0 in range(0, nrow, CHUNK):
+            v = scaled[l, r0 + 2 : r0 + 2 + CHUNK].reshape(CHUNK * nprobe, 128)
+            cols = lax.dot_general(
+                jnp.concatenate(halves(v), axis=1), ring[...], (((1,), (0,)), ((), ())), preferred_element_type=F32
+            )
+            for r in range(r0, r0 + CHUNK):
+                at = slice((r - r0) * nprobe, (r - r0 + 1) * nprobe)
+                c = [wide(co[f, l, r], nprobe) for f in range(NF)]
+                t = c[CEN] * scaled[l, r + 2] + 0.2 * (scaled[above, r + 2] + scaled[below, r + 2])
+                if r + 1 < nrow:
+                    t = t + c[XP] * scaled[l, r + 3]
+                if r >= 1:
+                    t = t + c[XM] * scaled[l, r + 1]
+                if r >= 2 and r + 2 < nrow:
+                    t = t + c[XA] * (scaled[l, r] - scaled[l, r + 4])
+                elif r >= 2:
+                    t = t + c[XA] * scaled[l, r]
+                else:
+                    t = t - c[XA] * scaled[l, r + 4]
+                t = t + c[YA] * cols[at, :128] + c[DIF] * cols[at, 128:]
+                tang[l, r] = t
+                if 2 <= r < nrow - 2:
+                    acc = put(acc, r, t)
         strip[l] = acc
         return carry
 
-    lax.fori_loop(0, nlev, tangent_inner, 0)
-    lax.fori_loop(0, nlev, gather, 0)
+    lax.fori_loop(0, nlev, tangent_own, 0, unroll=2)
 
     def tangent_outer(l):
         e1 = edge[0, pl.ds(l, 1), :]
@@ -253,15 +277,22 @@
         corr = e1 * near + ea * far
         acc = strip[l] + corr
         ends = {}
-        for r in (0, 1, nrow - 2, nrow - 1):
-            t = tangent_row(l, r) + take(corr, r)
+        last = nrow - 1
+
+        def coef(f, r):
+            return wide(co[f, l, r], nprobe)
+
+        rim_terms = {
+            0: coef(XM, 0) * scaled[l, 1] + coef(XA, 0) * scaled[l, 0],
+            1: coef(XA, 1) * scaled[l, 1],
+            last - 1: -(coef(XA, last - 1) * scaled[l, nrow + 2]),
+            last: coef(XP, last) * scaled[l, nrow + 2] - coef(XA, last) * scaled[l, nrow + 3],
+        }
+        for r in rim_terms:
+            t = tang[l, r] + rim_terms[r] + take(corr, r)
             tang[l, r] = t
             ends[r] = t
             acc = put(acc, r, t)
-        last = nrow - 1
-
-        def coef(f, r):
-            return wide(co[f, l, r], nprobe)
 
         to_low[l, 0] = coef(XA, 0) * ends[0]
         to_low[l, 1] = coef(XM, 0) * ends[0] + coef(XA, 1) * ends[1]
@@ -290,23 +321,33 @@
     def adjoint_own(l, carry):
         above = jnp.minimum(l + 1, nlev - 1)
         below = jnp.maximum(l - 1, 0)
-        for r in range(nrow):
-            c = [wide(co[f, l, r], nprobe) for f in (CEN, YP, YM, YA)]
-            w = tang[l, r]
-            b = c[0] * w + 0.2 * (tang[above, r] + tang[below, r])
-            if r + 1 < nrow:
-                b = b + wide(co[XM, l, r + 1], nprobe) * tang[l, r + 1]
-            if r >= 1:
-                b = b + wide(co[XP, l, r - 1], nprobe) * tang[l, r - 1]
-            if r + 2 < nrow:
-                b = b + wide(co[XA, l, r + 2], nprobe) * tang[l, r + 2]
-            if r >= 2:
-                b = b - wide(co[XA, l, r - 2], nprobe) * tang[l, r - 2]
-            ya = c[3] * w
-            back[l, r] = b + roll(c[2] * w, -1) + roll(c[1] * w, 1) + (roll(ya, -2) - roll(ya, 2))
-        return carry
-
-    lax.fori_loop(0, nlev, adjoint_own, 0)
+        for r0 in range(0, nrow, CHUNK):
+            parts = []
+            for r in range(r0, r0 + CHUNK):
+                w = tang[l, r]
+                parts.append(
+                    jnp.concatenate(
+                        halves(wide(co[DIF, l, r], nprobe) * w) + halves(wide(co[YA, l, r], nprobe) * w), axis=1
+                    )
+                )
+            cols = lax.dot_general(
+                jnp.concatenate(parts, axis=0), ring_t[...], (((1,), (0,)), ((), ())), preferred_element_type=F32
+            )
+            for r in range(r0, r0 + CHUNK):
+                b = cols[(r - r0) * nprobe : (r - r0 + 1) * nprobe]
+                b = b + wide(co[CEN, l, r], nprobe) * tang[l, r] + 0.2 * (tang[above, r] + tang[below, r])
+                if r + 1 < nrow:
+                    b = b + wide(co[XM, l, r + 1], nprobe) * tang[l, r + 1]
+                if r >= 1:
+                    b = b + wide(co[XP, l, r - 1], nprobe) * tang[l, r - 1]
+                if r + 2 < nrow:
+                    b = b + wide(co[XA, l, r + 2], nprobe) * tang[l, r + 2]
+                if r >= 2:
+                    b = b - wide(co[XA, l, r - 2], nprobe) * tang[l, r - 2]
+                back[l, r] = b
+        return carry
+
+    lax.fori_loop(0, nlev, adjoint_own, 0, unroll=2)
 
     def sketch_level(l):
         corr = jnp.where(quad < 2, wrap_r[l], wrap_l[l]) - wrap[l]
@@ -512,12 +553,14 @@
         scratch_shapes=[
             pltpu.VMEM((nprobe, nlev, nrow, ncol), BF16),
             pltpu.VMEM((4, nlev, nrow, ncol), F32),
-            pltpu.VMEM((nprobe * nrow, ncol), F32),
+            pltpu.VMEM((GROUP, nprobe * nrow, ncol), F32),
             pltpu.VMEM((nlev, nrow, nprobe, ncol), BF16),
             pltpu.VMEM((nlev, nrow + 4, nprobe, ncol), F32),
             pltpu.VMEM((nlev, nrow, nprobe, ncol), F32),
             pltpu.VMEM((NF, nlev, nrow, 8, ncol), F32),
             pltpu.VMEM((2, nlev, ncol), F32),
+            pltpu.VMEM((256, 256), BF16),
+            pltpu.VMEM((512, 128), BF16),
             strip, strip, strip, strip, strip, strip,
             rows2, rows2, rows2, rows2,
             pltpu.VMEM((nlev, nrow, nprobe, ncol), F32),

time: 40.6 us -> 40 us (0.985)
  Pallas kernels: 39.8 us -> 39.3 us
    pallas_call x1, Pallas kernels: 35.2 us -> 34.7 us  [shards(): pl.pallas_call(functools.partial(halo_kernel, (nprobe, nlev, nrow, nrd, n...]
where the time goes in v1:
time: 40 us; the launch traced here: 39.9 us
  Pallas kernels  39.3 us (98%)
  between operations  0.64 us (2%)
    pallas_call x1, Pallas kernels, shards(): pl.pallas_call(functools.partial(halo_kernel, (nprobe, nlev, nrow, nrd, n...  34.7 us
    pallas_call x1, Pallas kernels, shards(): pl.pallas_call(functools.partial(basis_kernel, nprobe, nlev, nrow, scale)...  4.62 us

profile of v1, /device:TPU:1, one launch (start us, length us, event | category | flops | bytes accessed | tf_op | source)
XLA Modules:
  0.0 39.9 jit_solution(7430164554862580605)
XLA Ops:
  0.6 34.7 %sketch_and_sums.1 = (bf16[8,16,64,128]{3,2,1,0:T(8,128)(2,1)S(1)}, f32[16,128]{1,0:T(8,128)S(1)}) custom-call(bf16[32,8,16,128]{3,2,1,0:T(8,128)(2,1)} %probes_hbm.1, f32[8,16,128]{2,1,0:T(8,128)} %spread_hbm.1, f32[8,16,128]{2,1,0:T(8,128)} %advx_hbm.1, f32[8,16,128]{2,1,0:T(8,128)} %advy_hbm.1, f32[8,16,128]{2,1,0:T(8,128)} %diff_hbm.1), custom_call_target="tpu_custom_call" | custom-call | tf_op jit(solution)/shard_map/sketch_and_sums/pallas_call | solution.py:545
  35.3 4.6 %factors_and_basis.1 = (f32[32,8,16,128]{3,2,1,0:T(8,128)}, f32[32,32]{1,0:T(8,128)}) custom-call(f32[16,128]{1,0:T(8,128)S(1)} %get-tuple-element.4.g_ref, bf16[8,16,64,128]{3,2,1,0:T(8,128)(2,1)S(1)} %get-tuple-element.5.z_hbm), custom_call_target="tpu_custom_call" | custom-call | tf_op jit(solution)/shard_map/factors_and_basis/pallas_call | solution.py:587

commit v2 on v1

--- a/solution.py
+++ b/solution.py
@@ -65,19 +65,25 @@
     chip = (row // 2) * INNER + xi
     plane = (nrd // 2) * INNER
 
-    def in_plane(t):
-        return ((t // INNER) * 2 + core, zi * INNER + lax.rem(t, INNER))
-
-    def in_line(t):
-        return (row, t * INNER + xi)
-
+    def far(o, count):
+        return min(o, count - o)
+
+    yi = row // 2
+    tall = nrd // 2
+    steps = [(dy, dx) for dy in range(tall) for dx in range(INNER)][1:]
+    steps.sort(key=lambda st: -(far(st[0], tall) + far(st[1], INNER)))
+    in_plane = [
+        (lax.rem(yi + dy, tall) * 2 + core, zi * INNER + lax.rem(xi + dx, INNER)) for dy, dx in steps
+    ]
+    in_line = [
+        (row, lax.rem(zi + o, outer) * INNER + xi) for o in sorted(range(1, outer), key=lambda o: -far(o, outer))
+    ]
     other = (row + 1 - 2 * core, col)
     barrier = pltpu.get_barrier_semaphore()
     greet = [other]
     greet += [(lax.rem(row + o, nrd), col) for o in (1, nrd - 1)]
     greet += [(row, lax.rem(col + o, ncd)) for o in (1, ncd - 1)]
-    greet += [in_plane(lax.rem(chip + o, plane)) for o in range(1, plane)]
-    greet += [in_line(lax.rem(zi + o, outer)) for o in range(1, outer)]
+    greet += in_plane + in_line
     for device in greet:
         pl.semaphore_signal(barrier, inc=1, device_id=device, device_id_type=MESH)
     signals = len(greet)
@@ -127,50 +133,53 @@
 
     has = {LOW: row > 0, HIGH: row < nrd - 1, LEFT: col > 0, RIGHT: col < ncd - 1}
     target = {LOW: (row - 1, col), HIGH: (row + 1, col), LEFT: (row, col - 1), RIGHT: (row, col + 1)}
+    def some(g):
+        return pl.ds(g * GROUP, GROUP)
+
     rims = (
         {
-            LOW: (lambda l: scaled.at[l, 2:4], lambda l: scaled.at[l, nrow + 2 : nrow + 4]),
-            HIGH: (lambda l: scaled.at[l, nrow : nrow + 2], lambda l: scaled.at[l, 0:2]),
-            LEFT: (lambda l: pack.at[l], lambda l: pack_r.at[l]),
-            RIGHT: (lambda l: pack.at[l], lambda l: pack_l.at[l]),
+            LOW: (lambda g: scaled.at[some(g), 2:4], lambda g: scaled.at[some(g), nrow + 2 : nrow + 4]),
+            HIGH: (lambda g: scaled.at[some(g), nrow : nrow + 2], lambda g: scaled.at[some(g), 0:2]),
+            LEFT: (lambda g: pack.at[some(g)], lambda g: pack_r.at[some(g)]),
+            RIGHT: (lambda g: pack.at[some(g)], lambda g: pack_l.at[some(g)]),
         },
         {
-            LOW: (lambda l: to_low.at[l], lambda l: from_high.at[l]),
-            HIGH: (lambda l: to_high.at[l], lambda l: from_low.at[l]),
-            LEFT: (lambda l: wrap.at[l], lambda l: wrap_r.at[l]),
-            RIGHT: (lambda l: wrap.at[l], lambda l: wrap_l.at[l]),
+            LOW: (lambda g: to_low.at[some(g)], lambda g: from_high.at[some(g)]),
+            HIGH: (lambda g: to_high.at[some(g)], lambda g: from_low.at[some(g)]),
+            LEFT: (lambda g: wrap.at[some(g)], lambda g: wrap_r.at[some(g)]),
+            RIGHT: (lambda g: wrap.at[some(g)], lambda g: wrap_l.at[some(g)]),
         },
     )
     opposite = {LOW: HIGH, HIGH: LOW, LEFT: RIGHT, RIGHT: LEFT}
 
-    def rim(phase, side, l):
+    def rim(phase, side, g):
         src, dst = rims[phase][side]
         return pltpu.make_async_remote_copy(
-            src_ref=src(l),
-            dst_ref=dst(l),
-            send_sem=send_sem.at[phase, side, l],
-            recv_sem=recv_sem.at[phase, side, l],
+            src_ref=src(g),
+            dst_ref=dst(g),
+            send_sem=send_sem.at[phase, side, g],
+            recv_sem=recv_sem.at[phase, side, g],
             device_id=target[side],
             device_id_type=MESH,
         )
 
-    def send(phase, l):
+    def send(phase, g):
         for side in (LOW, HIGH, LEFT, RIGHT):
             @pl.when(has[side])
             def _():
-                rim(phase, side, l).start()
-
-    def receive(phase, l):
+                rim(phase, side, g).start()
+
+    def receive(phase, g):
         for side in (LEFT, RIGHT, LOW, HIGH):
             @pl.when(has[side])
             def _():
-                rim(phase, opposite[side], l).wait_recv()
-
-    def sent(phase, l):
+                rim(phase, opposite[side], g).wait_recv()
+
+    def sent(phase, g):
         for side in (LOW, HIGH, LEFT, RIGHT):
             @pl.when(has[side])
             def _():
-                rim(phase, side, l).wait_send()
+                rim(phase, side, g).wait_send()
 
     zero_rows = jnp.zeros((nlev, 2, nprobe, 128), F32)
     zero_pack = jnp.zeros((nlev, half, 128), F32)
@@ -226,8 +235,7 @@
         group = [g * GROUP + i for i in range(GROUP)]
         for i, l in enumerate(group):
             scale_level(l, turn.at[i])
-        for l in group:
-            send(0, l)
+        send(0, g)
         return carry
 
     lax.fori_loop(0, nlev // GROUP, scale_group, 0)
@@ -308,12 +316,10 @@
 
     def tangent_rims(g, carry):
         group = [g * GROUP + i for i in range(GROUP)]
-        for l in group:
-            receive(0, l)
+        receive(0, g)
         for l in group:
             tangent_outer(l)
-        for l in group:
-            send(1, l)
+        send(1, g)
         return carry
 
     lax.fori_loop(0, nlev // GROUP, tangent_rims, 0)
@@ -375,12 +381,10 @@
 
     def sketch_rims(g, gram):
         group = [g * GROUP + i for i in range(GROUP)]
-        for l in group:
-            receive(1, l)
+        receive(1, g)
         for l in group:
             gram = gram + sketch_level(l)
-        for l in group:
-            pltpu.make_async_copy(zbuf.at[l], z_hbm.at[l], out_sem.at[l]).start()
+        pltpu.make_async_copy(zbuf.at[some(g)], z_hbm.at[some(g)], out_sem.at[g]).start()
         return gram
 
     gram = lax.fori_loop(0, nlev // GROUP, sketch_rims, jnp.zeros((2 * nprobe, 2 * nprobe), F32))
@@ -404,49 +408,51 @@
     quarter = half // 2
     mine = pl.ds(pl.multiple_of(core * quarter, quarter), quarter)
     part = pair_part[0, mine] + pair_part[1, mine]
-    copies = [swap]
-    for s, (buf, count, me, at) in enumerate(((red_b, plane, chip, in_plane), (red_c, outer, zi, in_line))):
+
+    def finish(g, carry):
+        sent(0, g)
+        sent(1, g)
+        pltpu.make_async_copy(zbuf.at[some(g)], z_hbm.at[some(g)], out_sem.at[g]).wait()
+        return carry
+
+    pending = [swap]
+    for s, (buf, count, me, reach) in enumerate(((red_b, plane, chip, in_plane), (red_c, outer, zi, in_line))):
         buf[me] = part
         stage = []
-        for o in range(1, count):
+        for o, device in enumerate(reach):
             stage.append(
                 pltpu.make_async_remote_copy(
                     src_ref=buf.at[me],
                     dst_ref=buf.at[me],
                     send_sem=red_send.at[s + 1, o],
                     recv_sem=red_recv.at[s + 1, o],
-                    device_id=at(lax.rem(me + o, count)),
+                    device_id=device,
                     device_id_type=MESH,
                 )
             )
             stage[-1].start()
-        for copy in stage:
+        if s == 0:
+            lax.fori_loop(0, nlev // GROUP, finish, 0)
+        for copy in pending:
+            copy.wait_send()
+        pending = stage
+        for copy in reversed(stage):
             copy.wait_recv()
         terms = [buf[o] for o in range(count)]
         while len(terms) > 1:
             terms = [sum(terms[i : i + 2][1:], terms[i]) for i in range(0, len(terms), 2)]
         part = terms[0]
-        copies += stage
     total[mine] = part
     join = pltpu.make_async_remote_copy(
         src_ref=total.at[mine], dst_ref=total.at[mine], send_sem=red_send.at[0, 1], recv_sem=red_recv.at[0, 1],
         device_id=other, device_id_type=MESH,
     )
     join.start()
+    for copy in pending:
+        copy.wait_send()
     join.wait_recv()
-    copies.append(join)
     g_ref[...] = total[...]
-
-    for copy in copies:
-        copy.wait_send()
-
-    def finish(l, carry):
-        sent(0, l)
-        sent(1, l)
-        pltpu.make_async_copy(zbuf.at[l], z_hbm.at[l], out_sem.at[l]).wait()
-        return carry
-
-    lax.fori_loop(0, nlev, finish, 0)
+    join.wait_send()
 
 
 def basis_kernel(nprobe, nlev, nrow, scale, g_ref, z_hbm, basis_hbm, factor_ref, zbuf, obuf, in_sem, out_sem):
@@ -572,9 +578,9 @@
             pltpu.VMEM((ncd // INNER, half // 2, ncol), F32),
             pltpu.VMEM((half, ncol), F32),
             pltpu.SemaphoreType.DMA((5,)),
-            pltpu.SemaphoreType.DMA((nlev,)),
-            pltpu.SemaphoreType.DMA((2, 4, nlev)),
-            pltpu.SemaphoreType.DMA((2, 4, nlev)),
+            pltpu.SemaphoreType.DMA((nlev // GROUP,)),
+            pltpu.SemaphoreType.DMA((2, 4, nlev // GROUP)),
+            pltpu.SemaphoreType.DMA((2, 4, nlev // GROUP)),
             pltpu.SemaphoreType.DMA((3, most)),
             pltpu.SemaphoreType.DMA((3, most)),
         ],

time: 40 us -> 38.9 us (0.972)
  Pallas kernels: 39.3 us -> 38.1 us
    pallas_call x1, Pallas kernels: 34.7 us -> 33.5 us  [shards(): pl.pallas_call(functools.partial(halo_kernel, (nprobe, nlev, nrow, nrd, n...]
where the time goes in v2:
time: 38.9 us; the launch traced here: 38.8 us
  Pallas kernels  38.1 us (98%)
  between operations  0.64 us (2%)
    pallas_call x1, Pallas kernels, shards(): pl.pallas_call(functools.partial(halo_kernel, (nprobe, nlev, nrow, nrd, n...  33.5 us
    pallas_call x1, Pallas kernels, shards(): pl.pallas_call(functools.partial(basis_kernel, nprobe, nlev, nrow, scale)...  4.63 us

profile of v2, /device:TPU:1, one launch (start us, length us, event | category | flops | bytes accessed | tf_op | source)
XLA Modules:
  0.0 38.8 jit_solution(10449336842252923861)
XLA Ops:
  0.6 33.5 %sketch_and_sums.1 = (bf16[8,16,64,128]{3,2,1,0:T(8,128)(2,1)S(1)}, f32[16,128]{1,0:T(8,128)S(1)}) custom-call(bf16[32,8,16,128]{3,2,1,0:T(8,128)(2,1)} %probes_hbm.1, f32[8,16,128]{2,1,0:T(8,128)} %spread_hbm.1, f32[8,16,128]{2,1,0:T(8,128)} %advx_hbm.1, f32[8,16,128]{2,1,0:T(8,128)} %advy_hbm.1, f32[8,16,128]{2,1,0:T(8,128)} %diff_hbm.1), custom_call_target="tpu_custom_call" | custom-call | tf_op jit(solution)/shard_map/sketch_and_sums/pallas_call | solution.py:551
  34.2 4.6 %factors_and_basis.1 = (f32[32,8,16,128]{3,2,1,0:T(8,128)}, f32[32,32]{1,0:T(8,128)}) custom-call(f32[16,128]{1,0:T(8,128)S(1)} %get-tuple-element.4.g_ref, bf16[8,16,64,128]{3,2,1,0:T(8,128)(2,1)S(1)} %get-tuple-element.5.z_hbm), custom_call_target="tpu_custom_call" | custom-call | tf_op jit(solution)/shard_map/factors_and_basis/pallas_call | solution.py:593

commit v3 on v2

--- a/solution.py
+++ b/solution.py
@@ -39,12 +39,12 @@
 def halo_kernel(
     dims,
     probes_hbm, spread_hbm, advx_hbm, advy_hbm, diff_hbm,
-    z_hbm, g_ref,
+    z_hbm, g_hbm,
     probes, coefs, turn, omega, scaled, tang, co, edge, ring, ring_t,
     pack, pack_l, pack_r, wrap, wrap_l, wrap_r,
     to_low, to_high, from_low, from_high,
     back, strip, zbuf, gbuf, red_a, red_b, red_c, total,
-    in_sem, out_sem, send_sem, recv_sem, red_send, red_recv,
+    in_sem, out_sem, send_sem, recv_sem, red_send, red_recv, news,
 ):
     nprobe, nlev, nrow, nrd, ncd = dims
     outer = ncd // INNER
@@ -83,10 +83,22 @@
     greet = [other]
     greet += [(lax.rem(row + o, nrd), col) for o in (1, nrd - 1)]
     greet += [(row, lax.rem(col + o, ncd)) for o in (1, ncd - 1)]
-    greet += in_plane + in_line
+    next_x = [(row, zi * INNER + lax.rem(xi + o, INNER)) for o in (1, INNER - 1)]
+    next_y = [(lax.rem(yi + o, tall) * 2 + core, col) for o in (1, tall - 1)]
+    next_z = [(row, lax.rem(zi + o, outer) * INNER + xi) for o in (1, outer - 1)]
+    skip_z = [(row, lax.rem(zi + o, outer) * INNER + xi) for o in (2, outer - 2)]
+    greet += next_x + next_y + next_z
     for device in greet:
         pl.semaphore_signal(barrier, inc=1, device_id=device, device_id_type=MESH)
     signals = len(greet)
+
+    def tell(n, devices):
+        for device in devices:
+            pl.semaphore_signal(news.at[n], inc=1, device_id=device, device_id_type=MESH)
+
+    def hear(n):
+        pl.semaphore_wait(news.at[n], 2)
+
 
     for load in loads[:4]:
         load.wait()
@@ -239,6 +251,8 @@
         return carry
 
     lax.fori_loop(0, nlev // GROUP, scale_group, 0)
+    tell(0, next_x)
+    tell(1, next_z)
 
     def halves(x):
         high = x.astype(BF16)
@@ -275,6 +289,10 @@
         return carry
 
     lax.fori_loop(0, nlev, tangent_own, 0, unroll=2)
+    hear(0)
+    hear(1)
+    tell(2, next_y)
+    tell(3, skip_z)
 
     def tangent_outer(l):
         e1 = edge[0, pl.ds(l, 1), :]
@@ -323,6 +341,9 @@
         return carry
 
     lax.fori_loop(0, nlev // GROUP, tangent_rims, 0)
+    hear(2)
+    hear(3)
+    tell(4, next_y)
 
     def adjoint_own(l, carry):
         above = jnp.minimum(l + 1, nlev - 1)
@@ -354,6 +375,7 @@
         return carry
 
     lax.fori_loop(0, nlev, adjoint_own, 0, unroll=2)
+    hear(4)
 
     def sketch_level(l):
         corr = jnp.where(quad < 2, wrap_r[l], wrap_l[l]) - wrap[l]
@@ -444,28 +466,33 @@
         part = terms[0]
     total[mine] = part
     join = pltpu.make_async_remote_copy(
-        src_ref=total.at[mine], dst_ref=total.at[mine], send_sem=red_send.at[0, 1], recv_sem=red_recv.at[0, 1],
+        src_ref=total.at[mine], dst_ref=g_hbm.at[mine], send_sem=red_send.at[0, 1], recv_sem=red_recv.at[0, 1],
         device_id=other, device_id_type=MESH,
     )
     join.start()
+    keep = pltpu.make_async_copy(total.at[mine], g_hbm.at[mine], in_sem.at[0])
+    keep.start()
     for copy in pending:
         copy.wait_send()
+    keep.wait()
+    join.wait_send()
     join.wait_recv()
-    g_ref[...] = total[...]
-    join.wait_send()
-
-
-def basis_kernel(nprobe, nlev, nrow, scale, g_ref, z_hbm, basis_hbm, factor_ref, zbuf, obuf, in_sem, out_sem):
+
+
+def basis_kernel(nprobe, nlev, nrow, scale, g_hbm, z_hbm, basis_hbm, factor_hbm, gbuf, zbuf, obuf, fbuf, in_sem, out_sem):
     def load(l):
         return pltpu.make_async_copy(z_hbm.at[l], zbuf.at[l], in_sem.at[l])
 
     def store(l):
         return pltpu.make_async_copy(obuf.at[l], basis_hbm.at[:, l], out_sem.at[l])
 
+    sums = pltpu.make_async_copy(g_hbm, gbuf, in_sem.at[nlev])
+    sums.start()
     for l in range(nlev):
         load(l).start()
     half = nprobe // 2
-    g = g_ref[...]
+    sums.wait()
+    g = gbuf[...]
     both = jnp.concatenate([g, roll(g, 64)], axis=0)
     flip = both.T
     lane = lanes((nprobe, 128))
@@ -504,7 +531,9 @@
     factor = lax.dot_general(
         upper, inv_c, (((1,), (1,)), ((), ())), precision=lax.Precision.HIGHEST, preferred_element_type=F32
     )
-    factor_ref[...] = factor
+    fbuf[...] = factor
+    leave = pltpu.make_async_copy(fbuf, factor_hbm, out_sem.at[nlev])
+    leave.start()
     a = inv_g * scale
     a_hi = a.astype(BF16)
     a_lo = (a - a_hi.astype(F32)).astype(BF16)
@@ -534,6 +563,7 @@
         return carry
 
     lax.fori_loop(0, nlev, finish, 0)
+    leave.wait()
 
 
 def shards(probes, spread, adv_x, adv_y, diffusivity):
@@ -542,8 +572,7 @@
     ncd = lax.axis_size("col")
     half = nprobe // 2
     inputs = [pltpu.with_memory_space_constraint(x, pltpu.HBM) for x in (probes, spread, adv_x, adv_y, diffusivity)]
-    any_spec = pl.BlockSpec(memory_space=pltpu.HBM)
-    vmem_spec = pl.BlockSpec(memory_space=pltpu.VMEM)
+    any_spec = pl.BlockSpec(memory_space=pl.ANY)
     rows2 = pltpu.VMEM((nlev, 2, nprobe, ncol), F32)
     strip = pltpu.VMEM((nlev, half, ncol), F32)
     plane = (nrd // 2) * INNER
@@ -555,7 +584,7 @@
             jax.ShapeDtypeStruct((half, ncol), F32),
         ),
         in_specs=[any_spec] * 5,
-        out_specs=(any_spec, vmem_spec),
+        out_specs=(any_spec, any_spec),
         scratch_shapes=[
             pltpu.VMEM((nprobe, nlev, nrow, ncol), BF16),
             pltpu.VMEM((4, nlev, nrow, ncol), F32),
@@ -583,6 +612,7 @@
             pltpu.SemaphoreType.DMA((2, 4, nlev // GROUP)),
             pltpu.SemaphoreType.DMA((3, most)),
             pltpu.SemaphoreType.DMA((3, most)),
+            pltpu.SemaphoreType.REGULAR((5,)),
         ],
         compiler_params=pltpu.CompilerParams(
             collective_id=0, has_side_effects=True, vmem_limit_bytes=40 * 1024 * 1024
@@ -596,13 +626,15 @@
             jax.ShapeDtypeStruct((nprobe, nlev, nrow, ncol), F32),
             jax.ShapeDtypeStruct((nprobe, nprobe), F32),
         ),
-        in_specs=[vmem_spec, any_spec],
-        out_specs=(any_spec, vmem_spec),
+        in_specs=[any_spec, any_spec],
+        out_specs=(any_spec, any_spec),
         scratch_shapes=[
+            pltpu.VMEM((half, ncol), F32),
             pltpu.VMEM((nlev, nrow, 2 * nprobe, ncol), BF16),
             pltpu.VMEM((nlev, nprobe, nrow, ncol), F32),
-            pltpu.SemaphoreType.DMA((nlev,)),
-            pltpu.SemaphoreType.DMA((nlev,)),
+            pltpu.VMEM((nprobe, nprobe), F32),
+            pltpu.SemaphoreType.DMA((nlev + 1,)),
+            pltpu.SemaphoreType.DMA((nlev + 1,)),
         ],
         compiler_params=pltpu.CompilerParams(vmem_limit_bytes=24 * 1024 * 1024),
         name="factors_and_basis",

time: 38.9 us -> 37.7 us (0.969)
  Pallas kernels: 38.1 us -> 37 us
    pallas_call x1, Pallas kernels: 33.5 us -> 32.9 us  [shards(): pl.pallas_call(functools.partial(halo_kernel, (nprobe, nlev, nrow, nrd, n...]
    pallas_call x1, Pallas kernels: 4.63 us -> 4.05 us  [shards(): pl.pallas_call(functools.partial(basis_kernel, nprobe, nlev, nrow, scale)...]
where the time goes in v3:
time: 37.7 us; the launch traced here: 37.6 us
  Pallas kernels  37 us (98%)
  between operations  0.64 us (2%)
    pallas_call x1, Pallas kernels, shards(): pl.pallas_call(functools.partial(halo_kernel, (nprobe, nlev, nrow, nrd, n...  32.9 us
    pallas_call x1, Pallas kernels, shards(): pl.pallas_call(functools.partial(basis_kernel, nprobe, nlev, nrow, scale)...  4.05 us

profile of v3, /device:TPU:1, one launch (start us, length us, event | category | flops | bytes accessed | tf_op | source)
XLA Modules:
  0.0 37.6 jit_solution(11803757893676902289)
XLA Ops:
  0.6 32.9 %sketch_and_sums.1 = (bf16[8,16,64,128]{3,2,1,0:T(8,128)(2,1)S(1)}, f32[16,128]{1,0:T(8,128)S(1)}) custom-call(bf16[32,8,16,128]{3,2,1,0:T(8,128)(2,1)} %probes_hbm.1, f32[8,16,128]{2,1,0:T(8,128)} %spread_hbm.1, f32[8,16,128]{2,1,0:T(8,128)} %advx_hbm.1, f32[8,16,128]{2,1,0:T(8,128)} %advy_hbm.1, f32[8,16,128]{2,1,0:T(8,128)} %diff_hbm.1), custom_call_target="tpu_custom_call" | custom-call | tf_op jit(solution)/shard_map/sketch_and_sums/pallas_call | solution.py:580
  33.5 4.1 %factors_and_basis.1 = (f32[32,8,16,128]{3,2,1,0:T(8,128)}, f32[32,32]{1,0:T(8,128)}) custom-call(f32[16,128]{1,0:T(8,128)S(1)} %get-tuple-element.4.g_hbm, bf16[8,16,64,128]{3,2,1,0:T(8,128)(2,1)S(1)} %get-tuple-element.5.z_hbm), custom_call_target="tpu_custom_call" | custom-call | tf_op jit(solution)/shard_map/factors_and_basis/pallas_call | solution.py:623

commit v4 on v3

--- a/solution.py
+++ b/solution.py
@@ -54,13 +54,6 @@
     xi = lax.rem(col, INNER)
     half = nprobe // 2
 
-    loads = []
-    for i, src in enumerate((spread_hbm, advx_hbm, advy_hbm, diff_hbm)):
-        loads.append(pltpu.make_async_copy(src, coefs.at[i], in_sem.at[i]))
-    loads.append(pltpu.make_async_copy(probes_hbm, probes, in_sem.at[4]))
-    for load in loads:
-        load.start()
-
     core = lax.rem(row, 2)
     chip = (row // 2) * INNER + xi
     plane = (nrd // 2) * INNER
@@ -80,17 +73,31 @@
     ]
     other = (row + 1 - 2 * core, col)
     barrier = pltpu.get_barrier_semaphore()
-    greet = [other]
+    greet = [(row, lax.rem(col + o, ncd)) for o in (1, ncd - 1)]
     greet += [(lax.rem(row + o, nrd), col) for o in (1, nrd - 1)]
-    greet += [(row, lax.rem(col + o, ncd)) for o in (1, ncd - 1)]
     next_x = [(row, zi * INNER + lax.rem(xi + o, INNER)) for o in (1, INNER - 1)]
     next_y = [(lax.rem(yi + o, tall) * 2 + core, col) for o in (1, tall - 1)]
     next_z = [(row, lax.rem(zi + o, outer) * INNER + xi) for o in (1, outer - 1)]
     skip_z = [(row, lax.rem(zi + o, outer) * INNER + xi) for o in (2, outer - 2)]
-    greet += next_x + next_y + next_z
+    greet += next_z + next_y + next_x + [other]
     for device in greet:
         pl.semaphore_signal(barrier, inc=1, device_id=device, device_id_type=MESH)
     signals = len(greet)
+
+    loads = []
+    for i, src in enumerate((spread_hbm, advx_hbm, advy_hbm, diff_hbm)):
+        loads.append(pltpu.make_async_copy(src, coefs.at[i], in_sem.at[i]))
+
+    gbuf[...] = jnp.zeros(gbuf.shape, F32)
+
+    def probe_load(g):
+        at = pl.ds(g * GROUP, GROUP)
+        return pltpu.make_async_copy(probes_hbm.at[:, at], probes.at[:, at], in_sem.at[4 + g])
+
+    for g in range(nlev // GROUP):
+        loads.append(probe_load(g))
+    for load in loads:
+        load.start()
 
     def tell(n, devices):
         for device in devices:
@@ -128,8 +135,10 @@
 
     pa = packed(2) * (1.0 / 12.0)
     pd = packed(3)
-    edge[0] = jnp.where(quad_l == 1, pd + 8.0 * pa, jnp.where(quad_l == 2, pd - 8.0 * pa, 0.0))
-    edge[1] = pa
+    near_edge = jnp.where(quad_l == 1, pd + 8.0 * pa, jnp.where(quad_l == 2, pd - 8.0 * pa, 0.0))
+    for l in range(nlev):
+        edge[0, l] = jnp.broadcast_to(near_edge[l : l + 1], (8, 128))
+        edge[1, l] = jnp.broadcast_to(pa[l : l + 1], (8, 128))
 
     for k, shape in enumerate(((256, 256), (512, 128))):
         src_lane = lax.rem(lax.broadcasted_iota(jnp.int32, shape, 0), 128)
@@ -144,7 +153,12 @@
             ring_t[...] = jnp.where(src_part < 2, both, -first).astype(BF16)
 
     has = {LOW: row > 0, HIGH: row < nrd - 1, LEFT: col > 0, RIGHT: col < ncd - 1}
-    target = {LOW: (row - 1, col), HIGH: (row + 1, col), LEFT: (row, col - 1), RIGHT: (row, col + 1)}
+    target = {
+        LOW: (lax.rem(row + nrd - 1, nrd), col),
+        HIGH: (lax.rem(row + 1, nrd), col),
+        LEFT: (row, lax.rem(col + ncd - 1, ncd)),
+        RIGHT: (row, lax.rem(col + 1, ncd)),
+    }
     def some(g):
         return pl.ds(g * GROUP, GROUP)
 
@@ -176,7 +190,7 @@
         )
 
     def send(phase, g):
-        for side in (LOW, HIGH, LEFT, RIGHT):
+        for side in (LEFT, RIGHT, LOW, HIGH):
             @pl.when(has[side])
             def _():
                 rim(phase, side, g).start()
@@ -216,8 +230,6 @@
         pack_r[...] = zero_pack
         wrap_r[...] = zero_pack
 
-    loads[4].wait()
-    pl.semaphore_wait(barrier, signals)
 
     def put(acc, r, value):
         slot = lax.div(lane16, 4)
@@ -243,14 +255,21 @@
             acc = put(acc, r, v)
         pack[l] = acc
 
-    def scale_group(g, carry):
-        group = [g * GROUP + i for i in range(GROUP)]
-        for i, l in enumerate(group):
-            scale_level(l, turn.at[i])
+    def scale_group(g):
+        probe_load(g).wait()
+        for i in range(GROUP):
+            scale_level(g * GROUP + i, turn.at[i])
+
+    scale_group(0)
+    pl.semaphore_wait(barrier, signals)
+    send(0, 0)
+
+    def scale_next(g, carry):
+        scale_group(g)
         send(0, g)
         return carry
 
-    lax.fori_loop(0, nlev // GROUP, scale_group, 0)
+    lax.fori_loop(1, nlev // GROUP, scale_next, 0)
     tell(0, next_x)
     tell(1, next_z)
 
@@ -295,8 +314,8 @@
     tell(3, skip_z)
 
     def tangent_outer(l):
-        e1 = edge[0, pl.ds(l, 1), :]
-        ea = edge[1, pl.ds(l, 1), :]
+        e1 = wide(edge[0, l], half)
+        ea = wide(edge[1, l], half)
         diff = jnp.where(quad < 2, pack_l[l], pack_r[l]) - pack[l]
         near = jnp.where(quad == 1, roll(diff, -1), roll(diff, 1))
         far = jnp.where(quad < 2, -roll(diff, -2), roll(diff, 2))
@@ -411,7 +430,6 @@
 
     gram = lax.fori_loop(0, nlev // GROUP, sketch_rims, jnp.zeros((2 * nprobe, 2 * nprobe), F32))
 
-    gbuf[...] = jnp.zeros(gbuf.shape, F32)
     gbuf[:, 0 : 2 * nprobe] = gram
     full = gbuf[...]
     high, probe = full[:nprobe], full[nprobe:]
@@ -438,7 +456,7 @@
         return carry
 
     pending = [swap]
-    for s, (buf, count, me, reach) in enumerate(((red_b, plane, chip, in_plane), (red_c, outer, zi, in_line))):
+    for s, (buf, count, me, reach) in enumerate(((red_c, outer, zi, in_line), (red_b, plane, chip, in_plane))):
         buf[me] = part
         stage = []
         for o, device in enumerate(reach):
@@ -593,7 +611,7 @@
             pltpu.VMEM((nlev, nrow + 4, nprobe, ncol), F32),
             pltpu.VMEM((nlev, nrow, nprobe, ncol), F32),
             pltpu.VMEM((NF, nlev, nrow, 8, ncol), F32),
-            pltpu.VMEM((2, nlev, ncol), F32),
+            pltpu.VMEM((2, nlev, 8, ncol), F32),
             pltpu.VMEM((256, 256), BF16),
             pltpu.VMEM((512, 128), BF16),
             strip, strip, strip, strip, strip, strip,
@@ -606,7 +624,7 @@
             pltpu.VMEM((plane, half // 2, ncol), F32),
             pltpu.VMEM((ncd // INNER, half // 2, ncol), F32),
             pltpu.VMEM((half, ncol), F32),
-            pltpu.SemaphoreType.DMA((5,)),
+            pltpu.SemaphoreType.DMA((4 + nlev // GROUP,)),
             pltpu.SemaphoreType.DMA((nlev // GROUP,)),
             pltpu.SemaphoreType.DMA((2, 4, nlev // GROUP)),
             pltpu.SemaphoreType.DMA((2, 4, nlev // GROUP)),

time: 37.7 us -> 37.5 us (level)
  no operation moved by 1% of the time
where the time goes in v4:
time: 37.5 us; the launch traced here: 37.4 us
  Pallas kernels  36.8 us (98%)
  between operations  0.64 us (2%)
    pallas_call x1, Pallas kernels, shards(): pl.pallas_call(functools.partial(halo_kernel, (nprobe, nlev, nrow, nrd, n...  32.7 us
    pallas_call x1, Pallas kernels, shards(): pl.pallas_call(functools.partial(basis_kernel, nprobe, nlev, nrow, scale)...  4.05 us

profile of v4, /device:TPU:1, one launch (start us, length us, event | category | flops | bytes accessed | tf_op | source)
XLA Modules:
  0.0 37.4 jit_solution(17164223900767915318)
XLA Ops:
  0.6 32.7 %sketch_and_sums.1 = (bf16[8,16,64,128]{3,2,1,0:T(8,128)(2,1)S(1)}, f32[16,128]{1,0:T(8,128)S(1)}) custom-call(bf16[32,8,16,128]{3,2,1,0:T(8,128)(2,1)} %probes_hbm.1, f32[8,16,128]{2,1,0:T(8,128)} %spread_hbm.1, f32[8,16,128]{2,1,0:T(8,128)} %advx_hbm.1, f32[8,16,128]{2,1,0:T(8,128)} %advy_hbm.1, f32[8,16,128]{2,1,0:T(8,128)} %diff_hbm.1), custom_call_target="tpu_custom_call" | custom-call | tf_op jit(solution)/shard_map/sketch_and_sums/pallas_call | solution.py:598
  33.4 4.0 %factors_and_basis.1 = (f32[32,8,16,128]{3,2,1,0:T(8,128)}, f32[32,32]{1,0:T(8,128)}) custom-call(f32[16,128]{1,0:T(8,128)S(1)} %get-tuple-element.4.g_hbm, bf16[8,16,64,128]{3,2,1,0:T(8,128)(2,1)S(1)} %get-tuple-element.5.z_hbm), custom_call_target="tpu_custom_call" | custom-call | tf_op jit(solution)/shard_map/factors_and_basis/pallas_call | solution.py:641

commit v5 on v4

--- a/solution.py
+++ b/solution.py
@@ -348,15 +348,16 @@
         wrap[l] = jnp.where(quad < 2, roll(u, -2), -roll(u, 2)) + jnp.where(
             quad == 1, roll(w, -1), jnp.where(quad == 2, roll(w, 1), 0.0)
         )
-        for r in range(2, nrow - 2):
-            tang[l, r] = tang[l, r] + take(corr, r)
+        return corr
 
     def tangent_rims(g, carry):
         group = [g * GROUP + i for i in range(GROUP)]
         receive(0, g)
-        for l in group:
-            tangent_outer(l)
+        corrs = [tangent_outer(l) for l in group]
         send(1, g)
+        for l, corr in zip(group, corrs):
+            for r in range(2, nrow - 2):
+                tang[l, r] = tang[l, r] + take(corr, r)
         return carry
 
     lax.fori_loop(0, nlev // GROUP, tangent_rims, 0)

time: 37.5 us -> 37.6 us (level)
  no operation moved by 1% of the time
where the time goes in v5:
time: 37.6 us; the launch traced here: 37.5 us
  Pallas kernels  36.8 us (98%)
  between operations  0.64 us (2%)
    pallas_call x1, Pallas kernels, shards(): pl.pallas_call(functools.partial(halo_kernel, (nprobe, nlev, nrow, nrd, n...  32.8 us
    pallas_call x1, Pallas kernels, shards(): pl.pallas_call(functools.partial(basis_kernel, nprobe, nlev, nrow, scale)...  4.05 us

profile of v5, /device:TPU:1, one launch (start us, length us, event | category | flops | bytes accessed | tf_op | source)
XLA Modules:
  0.0 37.5 jit_solution(1203563072753157473)
XLA Ops:
  0.6 32.8 %sketch_and_sums.1 = (bf16[8,16,64,128]{3,2,1,0:T(8,128)(2,1)S(1)}, f32[16,128]{1,0:T(8,128)S(1)}) custom-call(bf16[32,8,16,128]{3,2,1,0:T(8,128)(2,1)} %probes_hbm.1, f32[8,16,128]{2,1,0:T(8,128)} %spread_hbm.1, f32[8,16,128]{2,1,0:T(8,128)} %advx_hbm.1, f32[8,16,128]{2,1,0:T(8,128)} %advy_hbm.1, f32[8,16,128]{2,1,0:T(8,128)} %diff_hbm.1), custom_call_target="tpu_custom_call" | custom-call | tf_op jit(solution)/shard_map/sketch_and_sums/pallas_call | solution.py:599
  33.4 4.1 %factors_and_basis.1 = (f32[32,8,16,128]{3,2,1,0:T(8,128)}, f32[32,32]{1,0:T(8,128)}) custom-call(f32[16,128]{1,0:T(8,128)S(1)} %get-tuple-element.4.g_hbm, bf16[8,16,64,128]{3,2,1,0:T(8,128)(2,1)S(1)} %get-tuple-element.5.z_hbm), custom_call_target="tpu_custom_call" | custom-call | tf_op jit(solution)/shard_map/factors_and_basis/pallas_call | solution.py:642
